TPU v7x, 256 devices: a whole 4x4x8 slice. The times are simulated.
256 devices in a mesh: cross: 32 (over z, y), along: 8 (over x, core).
Axes of the slice: x: 4, y: 4, z: 8, core: 2. Of those that a mesh axis runs over, the one named last changes fastest.
Arguments:
- source: float32 [16, 128, 8192], P(None, 'along', 'cross'), may hold values from -6 to 6
- inv_density: float32 [16, 128, 8192], P(None, 'along', 'cross'), may hold values from 0.3 to 3
Outputs:
- pressure: float32 [16, 128, 8192], P(None, 'along', 'cross')
- residual: float32 [16, 128, 8192], P(None, 'along', 'cross')
All inputs are finite; a program needn't handle non-finite values.
Results may differ from a plain program's by a relative error of at most 0.0003.
Values sent between devices are 32-bit elements; how exact they have to be, the bound alone decides.
A program may use at most 128 MiB of HBM per device.

v0:
```python
import functools

import jax
import jax.numpy as jnp
from jax import lax
from jax.experimental import pallas as pl
from jax.experimental.pallas import tpu as pltpu
from jax.sharding import PartitionSpec as P

MESH = pl.DeviceIdType.MESH
SWEEPS = 4
NZ = 16
LANES = 128
FINE_ROWS = 32
COARSE_ROWS = 48
TINY = 1e-20

along_weight = 0.25
cross_weight = 1.0
vertical_weight = 0.5
relaxation = 0.8

COARSE_SIDES = [(d, e) for d in (0, 1, -1, 2, -2) for e in (0, 1, -1) if (d, e) != (0, 0)]
FINE_SIDES = [(d, e) for d in (0, 1, -1) for e in (0, 1, -1) if (d, e) != (0, 0)]


def layers(body, init, reverse=False):
    def step(i, carry):
        return body(NZ - 1 - i if reverse else i, carry)

    return lax.fori_loop(0, NZ, step, init, unroll=True)


def picked(values, lane_index):
    return jnp.take_along_axis(values, lane_index, axis=1, mode="promise_in_bounds")


def turned(values, by):
    return pltpu.roll(values, by % LANES, axis=1)


def row_turned(values, by):
    return pltpu.roll(values, by % values.shape[0], axis=0)


def harmonic(first, second):
    return 2.0 * first * second / jnp.maximum(first + second, TINY)


def lanes_of(rows):
    return lax.broadcasted_iota(jnp.int32, (rows, LANES), 1)


class Level:
    def __init__(self, phases, spread, rows, refs):
        self.phases, self.spread, self.rows = phases, spread, rows
        self.west, self.east, self.south, self.last_north, self.upper, self.inverse, self.link, self.value, self.forcing = refs

    @staticmethod
    def scratch(phases, rows):
        full = pltpu.VMEM((phases, NZ, rows, LANES), jnp.float32)
        return [
            full,
            full,
            full,
            pltpu.VMEM((NZ, rows, LANES), jnp.float32),
            pltpu.VMEM((phases, NZ + 1, rows, LANES), jnp.float32),
            full,
            full,
            full,
            full,
        ]

    def north(self, phase, k):
        return self.south[phase + 1, k] if phase + 1 < self.phases else self.last_north[k]

    def horizontal(self, k, values):
        out = []
        for phase, value in enumerate(values):
            before = values[phase - 1] if phase else turned(values[-1], self.spread)
            after = values[phase + 1] if phase + 1 < self.phases else turned(values[0], -self.spread)
            out.append(
                self.west[phase, k] * row_turned(value, 1)
                + self.east[phase, k] * row_turned(value, -1)
                + self.south[phase, k] * before
                + self.north(phase, k) * after
            )
        return out

    def set_faces(self, k, west, south, upper):
        for phase in range(self.phases):
            self.west[phase, k] = west[phase]
            self.east[phase, k] = row_turned(west[phase], -1)
            self.south[phase, k] = south[phase]
            self.upper[phase, k] = upper[phase]
        self.last_north[k] = turned(south[0], -self.spread)

    def close_upper(self):
        for phase in range(self.phases):
            self.upper[phase, NZ] = jnp.zeros((self.rows, LANES), jnp.float32)

    def factor(self, centre_ref=None):
        def body(k, before):
            now = []
            for phase in range(self.phases):
                upper, lower = self.upper[phase, k], self.upper[phase, k + 1]
                centre = self.west[phase, k] + self.east[phase, k] + self.south[phase, k] + self.north(phase, k) + upper + lower
                if centre_ref is not None:
                    centre_ref[phase, k] = centre
                inverse = 1.0 / jnp.maximum(centre - upper * upper * before[phase], TINY)
                self.inverse[phase, k] = inverse
                self.link[phase, k] = lower * inverse
                now.append(inverse)
            return tuple(now)

        zero = jnp.zeros((self.rows, LANES), jnp.float32)
        layers(body, (zero,) * self.phases)

    def start(self, held, after=None, low=0):
        rows = pl.ds(low, self.rows - low)
        zero = jnp.zeros((self.rows - low, LANES), jnp.float32)

        def down(k, before):
            now = []
            for phase in range(self.phases):
                total = self.forcing[phase, k, rows] + self.upper[phase, k, rows] * before[phase]
                now.append(total * self.inverse[phase, k, rows])
                held[phase, k, rows] = now[-1]
            return tuple(now)

        layers(down, (zero,) * self.phases)

        def up(k, below):
            now, values = [], []
            for phase in range(self.phases):
                now.append(held[phase, k, rows] + self.link[phase, k, rows] * below[phase])
                values.append(relaxation * now[-1])
                self.value[phase, k, rows] = values[-1]
            if after is not None:
                after(k, values)
            return tuple(now)

        layers(up, (zero,) * self.phases, reverse=True)

    def remain(self, k, values):
        return [(1.0 - relaxation) * self.forcing[phase, k] + part for phase, part in enumerate(self.horizontal(k, values))]

    def sweep(self, held, coarse=None):
        zero = jnp.zeros((self.rows, LANES), jnp.float32)

        def down(k, before):
            values = [self.value[phase, k] for phase in range(self.phases)]
            if coarse is not None:
                values = [value + extra for value, extra in zip(values, coarse(k))]
                for phase in range(self.phases):
                    self.value[phase, k] = values[phase]
            now = []
            for phase, part in enumerate(self.horizontal(k, values)):
                total = self.forcing[phase, k] + part + self.upper[phase, k] * before[phase]
                now.append(total * self.inverse[phase, k])
                held[phase, k] = now[-1]
            return tuple(now)

        layers(down, (zero,) * self.phases)

        def up(k, below):
            now = []
            for phase in range(self.phases):
                now.append(held[phase, k] + self.link[phase, k] * below[phase])
                self.value[phase, k] = (1.0 - relaxation) * self.value[phase, k] + relaxation * now[-1]
            return tuple(now)

        layers(up, (zero,) * self.phases, reverse=True)


def paired_lanes(values, spread, lane):
    return values + picked(values, lane ^ spread)


def first_child(values, spread, lane):
    return jnp.where((lane & spread) == 0, values, turned(values, spread))


def kernel(
    cross_count,
    along_count,
    source_ref,
    density_ref,
    pressure_ref,
    residual_ref,
    dense,
    first_out,
    last_out,
    first_in,
    last_in,
    near_out,
    far_out,
    own_in,
    near_in,
    far_in,
    fresh,
    cells,
    centre,
    held,
    coarse_held,
    *rest,
):
    level_refs, (fine_send, fine_recv, coarse_send, coarse_recv, fresh_send, fresh_recv) = rest[:-6], rest[-6:]
    shapes = [(4, 1, FINE_ROWS), (2, 1, FINE_ROWS), (1, 1, FINE_ROWS), (1, 2, FINE_ROWS), (1, 1, COARSE_ROWS), (1, 2, COARSE_ROWS), (1, 4, COARSE_ROWS)]
    grid = [Level(*shape, level_refs[9 * no : 9 * no + 9]) for no, shape in enumerate(shapes)]
    c, a = lax.axis_index("cross"), lax.axis_index("along")

    def inside(d, e):
        return (c + d >= 0) & (c + d < cross_count) & (a + e >= 0) & (a + e < along_count)

    for ref in (first_in, last_in, own_in, near_in, far_in, fresh):
        ref[...] = jnp.zeros(ref.shape, ref.dtype)
    dense[:, :, :, 16:32, :] = jnp.zeros((2, 2, NZ, 16, LANES), jnp.float32)

    barrier = pltpu.get_barrier_semaphore()
    for d, e in COARSE_SIDES:

        @pl.when(inside(d, e))
        def _(d=d, e=e):
            pl.semaphore_signal(barrier, inc=1, device_id=(c + d, a + e), device_id_type=MESH)

    def own_cells(which, ref):
        lane = lanes_of(16)
        index = (4 * (lane & 63) + (lane >> 6)) & 127
        lower = (lane & 63) < 32

        def body(k, _):
            left, right = ref[k, :, 0:LANES], ref[k, :, LANES : 2 * LANES]
            for half in range(2):
                at = index + 2 * half
                dense[which, half, k, 0:16] = jnp.where(lower, picked(left, at), picked(right, at))
            return 0

        layers(body, 0)
        slot = (lane & 63) >> 3
        for half in range(2):
            for group in range(2):
                first = last = jnp.zeros((16, LANES), jnp.float32)
                for q in range(8):
                    values = dense[which, half, 8 * group + q, 0:16]
                    first = jnp.where(slot == q, turned(values, 8 * q), first)
                    last = jnp.where(slot == q, turned(values, 8 * q + 72), last)
                first_out[which, half, group] = first
                last_out[which, half, group] = last

    def fine_copies(which):
        copies = []
        for no, (d, e) in enumerate(FINE_SIDES):
            rows_from = {0: (0, 16), 1: (0, 8), -1: (8, 16)}[e]
            rows_to = {0: (0, 16), 1: (16, 24), -1: (24, 32)}[e]
            take, put = pl.ds(rows_from[0], rows_from[1] - rows_from[0]), pl.ds(rows_to[0], rows_to[1] - rows_to[0])
            if d == 0:
                src, dst = dense.at[which, :, :, take, :], dense.at[which, :, :, put, :]
            elif d == 1:
                src, dst = first_out.at[which, :, :, take, :], first_in.at[which, :, :, put, :]
            else:
                src, dst = last_out.at[which, :, :, take, :], last_in.at[which, :, :, put, :]
            copies.append(
                (
                    d,
                    e,
                    pltpu.make_async_remote_copy(
                        src_ref=src,
                        dst_ref=dst,
                        send_sem=fine_send.at[which, no],
                        recv_sem=fine_recv.at[which, no],
                        device_id=(c - d, a - e),
                        device_id_type=MESH,
                    ),
                )
            )
        return copies

    def coarse_copies(which):
        fields = pl.ds(0, 3) if which == 0 else pl.ds(3, 1)
        copies = []
        for no, (d, e) in enumerate(COARSE_SIDES):
            put = pl.ds({0: 0, 1: 16, -1: 32}[e], 16)
            if d == 0:
                src, dst = own_in.at[fields, :, pl.ds(0, 16), :], own_in.at[fields, :, put, :]
            elif abs(d) == 1:
                side = 0 if d > 0 else 1
                src, dst = near_out.at[side, fields], near_in.at[side, fields, :, put, :]
            else:
                side = 0 if d > 0 else 1
                src, dst = far_out.at[fields], far_in.at[side, fields, put, :]
            copies.append(
                (
                    d,
                    e,
                    pltpu.make_async_remote_copy(
                        src_ref=src,
                        dst_ref=dst,
                        send_sem=coarse_send.at[which, no],
                        recv_sem=coarse_recv.at[which, no],
                        device_id=(c - d, a - e),
                        device_id_type=MESH,
                    ),
                )
            )
        return copies

    def fresh_copies():
        copies = []
        for no, (e, take) in enumerate([(1, 0), (-1, 8)]):
            copies.append(
                (
                    0,
                    e,
                    pltpu.make_async_remote_copy(
                        src_ref=grid[3].forcing.at[0, :, pl.ds(take, 8), :],
                        dst_ref=fresh.at[no],
                        send_sem=fresh_send.at[no],
                        recv_sem=fresh_recv.at[no],
                        device_id=(c, a - e),
                        device_id_type=MESH,
                    ),
                )
            )
        return copies

    def start(copies):
        for d, e, copy in copies:
            pl.when(inside(-d, -e))(copy.start)

    def arrive(copies):
        for d, e, copy in copies:
            pl.when(inside(d, e))(copy.wait_recv)

    def leave(copies):
        for d, e, copy in copies:
            pl.when(inside(-d, -e))(copy.wait_send)

    def whole_cells(which, target):
        lane = lanes_of(FINE_ROWS)
        own = lane < 64
        for group in range(2):
            halos = []
            for phase in range(4):
                first, last = first_in[which, phase // 2, group], last_in[which, phase // 2, group]
                if phase % 2 == 0:
                    halos.append(jnp.where(own, first, turned(last, 64)))
                else:
                    halos.append(jnp.where(own, turned(first, 64), last))

            def body(q, halos, group=group):
                index = jnp.where(lane < 96, (lane + 8 * q) & 63, 64 + ((lane + 8 + 8 * q) & 63))
                k = 8 * group + q
                for phase in range(4):
                    values = dense[which, phase // 2, k]
                    if phase % 2:
                        values = turned(values, 64)
                    target[phase, k] = jnp.where(own, values, picked(halos[phase], index))
                return halos

            lax.fori_loop(0, 8, body, tuple(halos), unroll=True)

    own_cells(1, density_ref)
    counted = (
        (jnp.minimum(c, 2) + jnp.minimum(cross_count - 1 - c, 2) + 1) * (jnp.minimum(a, 1) + jnp.minimum(along_count - 1 - a, 1) + 1) - 1
    )
    pl.semaphore_wait(barrier, counted)
    density_copies = fine_copies(1)
    start(density_copies)
    own_cells(0, source_ref)
    source_copies = fine_copies(0)
    start(source_copies)
    for level in grid:
        level.close_upper()
    arrive(density_copies)
    whole_cells(1, cells)

    lane = lanes_of(FINE_ROWS)
    lane_16 = lanes_of(16)

    def faces(k, above):
        now = [cells[phase, k] for phase in range(4)]
        west, south, upper = [], [], []
        for phase in range(4):
            before = now[phase - 1] if phase else turned(now[3], 1)
            west.append(along_weight * harmonic(now[phase], row_turned(now[phase], 1)))
            south.append(cross_weight * harmonic(now[phase], before))
            upper.append(vertical_weight * harmonic(now[phase], above[phase]))
        upper = [jnp.where(k == 0, 2.0 * vertical_weight * now[phase], upper[phase]) for phase in range(4)]
        grid[0].set_faces(k, west, south, upper)
        west, south, upper = [west[0] + west[1], west[2] + west[3]], [0.5 * south[0], 0.5 * south[2]], [upper[0] + upper[1], upper[2] + upper[3]]
        grid[1].set_faces(k, west, south, upper)
        west, south, upper = [west[0] + west[1]], [0.5 * south[0]], [upper[0] + upper[1]]
        grid[2].set_faces(k, west, south, upper)
        west, south, upper = paired_lanes(west[0], 1, lane), 0.5 * first_child(south[0], 1, lane), paired_lanes(upper[0], 1, lane)
        grid[3].set_faces(k, [west], [south], [upper])
        return tuple(now)

    layers(faces, (jnp.ones((FINE_ROWS, LANES), jnp.float32),) * 4)

    def pack(field, layer_of):
        near_index = 4 * (lane_16 & 15)
        far_index = 4 * ((lane_16 & 3) + 12 * (lane_16 >> 6))
        near_slot, far_slot = lane_16 >> 4, (lane_16 & 63) >> 2
        far = jnp.zeros((16, LANES), jnp.float32)
        for group in range(2):
            near = jnp.zeros((16, LANES), jnp.float32)
            for q in range(8):
                k = 8 * group + q
                value = layer_of(k)
                near = jnp.where(near_slot == q, value(near_index), near)
                far = jnp.where(far_slot == k, value(far_index), far)
            own_in[field, group, 0:16] = near
            near_out[0, field, group] = turned(near, 16)
            near_out[1, field, group] = turned(near, -16)
        far_out[field] = far

    def both(ref):
        def layer_of(k):
            values = ref[0, k, 0:16]
            return lambda index: picked(values, index) + picked(values, index + 2)

        return layer_of

    def half_first(ref):
        def layer_of(k):
            values = ref[0, k, 0:16]
            return lambda index: 0.5 * picked(values, index)

        return layer_of

    pack(0, both(grid[3].west))
    pack(1, half_first(grid[3].south))
    pack(2, both(grid[3].upper))
    face_copies = coarse_copies(0)
    start(face_copies)

    grid[0].factor(centre)
    for no in (1, 2, 3):
        grid[no].factor()

    arrive(source_copies)
    whole_cells(0, grid[0].forcing)

    def restrict(no):
        level, below = grid[no], grid[no + 1]

        def after(k, values):
            rest = level.remain(k, values)
            if level.phases > 1:
                for phase in range(below.phases):
                    below.forcing[phase, k] = rest[2 * phase] + rest[2 * phase + 1]
            else:
                below.forcing[0, k] = paired_lanes(rest[0], level.spread, lanes_of(level.rows))

        return after

    for no in (0, 1, 2):
        grid[no].start(held, restrict(no))
    third_copies = fresh_copies()
    start(third_copies)

    def keep_rest(k, values):
        cells[0, k] = grid[3].remain(k, values)[0]

    grid[3].start(held, keep_rest)
    pack(3, both(cells))
    forcing_copies = coarse_copies(1)
    start(forcing_copies)

    arrive(third_copies)

    def renew(k, _):
        grid[3].forcing[0, k, 16:24] = fresh[0, k]
        grid[3].forcing[0, k, 24:32] = fresh[1, k]
        return 0

    layers(renew, 0)
    grid[3].start(held, low=16)

    lane_48 = lanes_of(COARSE_ROWS)

    def unpacked(field):
        near_slot = lane_48 >> 4
        middle = (lane_48 >= 32) & (lane_48 < 112)
        far = jnp.where(lane_48 < 64, far_in[0, field], far_in[1, field])

        def layer_of(k):
            group, q = k // 8, k % 8
            mixed = jnp.where(
                near_slot == q,
                own_in[field, group],
                jnp.where(near_slot == (q + 1) % 8, near_in[0, field, group], near_in[1, field, group]),
            )
            index = jnp.where(lane_48 < 64, (4 * k + lane_48 + 32) & 63, 64 + ((4 * k + lane_48 + 20) & 63))
            return jnp.where(middle, picked(far, index), turned(mixed, -16 * q))

        return layer_of

    arrive(face_copies)
    west_of, south_of, upper_of = unpacked(0), unpacked(1), unpacked(2)
    for k in range(NZ):
        west, south, upper = west_of(k), south_of(k), upper_of(k)
        grid[4].set_faces(k, [west], [south], [upper])
        for no in (5, 6):
            spread = grid[no].spread // 2
            west, south, upper = paired_lanes(west, spread, lane_48), 0.5 * first_child(south, spread, lane_48), paired_lanes(upper, spread, lane_48)
            grid[no].set_faces(k, [west], [south], [upper])
    for no in (4, 5, 6):
        grid[no].factor()

    arrive(forcing_copies)
    forcing_of = unpacked(3)
    for k in range(NZ):
        grid[4].forcing[0, k] = forcing_of(k)

    grid[4].start(coarse_held, restrict(4))
    grid[5].start(coarse_held, restrict(5))
    grid[6].start(coarse_held)
    for _ in range(SWEEPS - 1):
        grid[6].sweep(coarse_held)
    grid[5].sweep(coarse_held, lambda k: [grid[6].value[0, k]])
    grid[4].sweep(coarse_held, lambda k: [grid[5].value[0, k]])

    def to_third(k):
        values = jnp.concatenate([grid[4].value[0, k, 0:24], grid[4].value[0, k, 40:48]], 0)
        return [picked(values, jnp.where(lane < 96, lane >> 2, (lane >> 2) + 96))]

    grid[3].sweep(held, to_third)
    grid[2].sweep(held, lambda k: [grid[3].value[0, k]])
    grid[1].sweep(held, lambda k: [grid[2].value[0, k]] * 2)
    grid[0].sweep(held, lambda k: [grid[1].value[phase // 2, k] for phase in range(4)])

    def laid_out(ref, k, phases):
        halves = [jnp.where(lane_16 < 64, phases[2 * half], turned(phases[2 * half + 1], 64)) for half in range(2)]
        index = (lane_16 & 1) * 64 + (lane_16 >> 2)
        for tile in range(2):
            at = index + 32 * tile
            ref[k, :, tile * LANES : (tile + 1) * LANES] = jnp.where((lane_16 & 3) < 2, picked(halves[0], at), picked(halves[1], at))

    fine = grid[0]

    def finish(k, above):
        values = [fine.value[phase, k] for phase in range(4)]
        next_k = jnp.minimum(k + 1, NZ - 1)
        rest = []
        for phase, part in enumerate(fine.horizontal(k, values)):
            own = pl.ds(0, 16)
            below = fine.value[phase, next_k, own]
            rest.append(
                fine.forcing[phase, k, own]
                - (
                    centre[phase, k, own] * values[phase][0:16]
                    - part[0:16]
                    - fine.upper[phase, k, own] * above[phase]
                    - fine.upper[phase, k + 1, own] * below
                )
            )
        values = [value[0:16] for value in values]
        laid_out(pressure_ref, k, values)
        laid_out(residual_ref, k, rest)
        return tuple(values)

    layers(finish, (jnp.zeros((16, LANES), jnp.float32),) * 4)

    for copies in (density_copies, source_copies, face_copies, third_copies, forcing_copies):
        leave(copies)


def solution(mesh):
    cross_count, along_count = mesh.shape["cross"], mesh.shape["along"]

    def per_device(source, density):
        shape = jax.ShapeDtypeStruct(source.shape, jnp.float32)
        vmem = lambda *dims: pltpu.VMEM(dims, jnp.float32)
        scratch = [
            vmem(2, 2, NZ, FINE_ROWS, LANES),
            vmem(2, 2, 2, 16, LANES),
            vmem(2, 2, 2, 16, LANES),
            vmem(2, 2, 2, FINE_ROWS, LANES),
            vmem(2, 2, 2, FINE_ROWS, LANES),
            vmem(2, 4, 2, 16, LANES),
            vmem(4, 16, LANES),
            vmem(4, 2, COARSE_ROWS, LANES),
            vmem(2, 4, 2, COARSE_ROWS, LANES),
            vmem(2, 4, COARSE_ROWS, LANES),
            vmem(2, NZ, 8, LANES),
            vmem(4, NZ, FINE_ROWS, LANES),
            vmem(4, NZ, FINE_ROWS, LANES),
            vmem(4, NZ, FINE_ROWS, LANES),
            vmem(1, NZ, COARSE_ROWS, LANES),
        ]
        for phases, rows in [(4, FINE_ROWS), (2, FINE_ROWS), (1, FINE_ROWS), (1, FINE_ROWS)] + [(1, COARSE_ROWS)] * 3:
            scratch += Level.scratch(phases, rows)
        scratch += [
            pltpu.SemaphoreType.DMA((2, len(FINE_SIDES))),
            pltpu.SemaphoreType.DMA((2, len(FINE_SIDES))),
            pltpu.SemaphoreType.DMA((2, len(COARSE_SIDES))),
            pltpu.SemaphoreType.DMA((2, len(COARSE_SIDES))),
            pltpu.SemaphoreType.DMA((2,)),
            pltpu.SemaphoreType.DMA((2,)),
        ]
        return pl.pallas_call(
            functools.partial(kernel, cross_count, along_count),
            out_shape=(shape, shape),
            in_specs=[pl.BlockSpec(memory_space=pltpu.VMEM)] * 2,
            out_specs=(pl.BlockSpec(memory_space=pltpu.VMEM),) * 2,
            scratch_shapes=scratch,
            compiler_params=pltpu.CompilerParams(collective_id=0, has_side_effects=True, vmem_limit_bytes=56 * 2**20),
        )(source, density)

    return jax.shard_map(
        per_device,
        mesh=mesh,
        in_specs=(P(None, "along", "cross"), P(None, "along", "cross")),
        out_specs=(P(None, "along", "cross"), P(None, "along", "cross")),
        check_vma=False,
    )
```

profile of v0, /device:TPU:131, one launch (start us, length us, event | category | flops | bytes accessed | tf_op | source)
XLA Modules:
  0.0 45.7 jit_solution(4344095791879643892)
XLA Ops:
  0.6 42.7 %shard_map.41 = (f32[16,16,256]{2,1,0:T(8,128)}, f32[16,16,256]{2,1,0:T(8,128)}) custom-call(f32[16,16,256]{2,1,0:T(8,128)} %source_ref.1, f32[16,16,256]{2,1,0:T(8,128)} %density_ref.1), custom_call_target="tpu_custom_call" | custom-call | tf_op jit(solution)/shard_map/pallas_call | solution.py:603
  43.3 0.0 copy-start
  43.3 1.7 %copy.6 = f32[16,16,256]{2,1,0:T(8,128)} copy(f32[16,16,256]{2,1,0:T(8,128)} %get-tuple-element.4) | data formatting | bytes 524288
  45.0 0.0 copy-done
  45.0 0.7 %copy.7 = f32[16,16,256]{2,1,0:T(8,128)} copy(f32[16,16,256]{2,1,0:T(8,128)S(1)} %copy-done) | data formatting | bytes 524288
Async XLA Ops:
  43.3 1.7 %copy-start = (f32[16,16,256]{2,1,0:T(8,128)S(1)}, f32[16,16,256]{2,1,0:T(8,128)}, u32[]{:S(2)}) copy-start(f32[16,16,256]{2,1,0:T(8,128)} %get-tuple-element.5) | copy-start | bytes 786436
where the time goes:
time: 46 us; the launch traced here: 45.7 us
  Pallas kernels  42.7 us (93%)
  local copies, waits for them, and re-layouts  2.42 us (5%)
  between operations  0.65 us (1%)
    pallas_call x1, Pallas kernels, per_device(): pl.pallas_call(functools.partial(kernel, cross_count, along_count), out_s...  42.7 us
    unnamed x4, local copies, waits for them, and re-layouts  2.42 us

commit v1 on v0

--- a/solution.py
+++ b/solution.py
@@ -12,7 +12,8 @@
 NZ = 16
 LANES = 128
 FINE_ROWS = 32
-COARSE_ROWS = 48
+COARSE_ROWS = 24
+HELD_ROWS = 48
 TINY = 1e-20
 
 along_weight = 0.25
@@ -51,25 +52,35 @@
     return lax.broadcasted_iota(jnp.int32, (rows, LANES), 1)
 
 
+def row_before(values, folded):
+    moved = row_turned(values, 1)
+    if not folded:
+        return moved
+    head = moved[0:8]
+    first = lax.broadcasted_iota(jnp.int32, head.shape, 0) == 0
+    return jnp.concatenate([jnp.where(first, turned(head, 64), head), moved[8:]], 0)
+
+
+def row_after(values, folded):
+    moved = row_turned(values, -1)
+    if not folded:
+        return moved
+    tail = moved[-8:]
+    last = lax.broadcasted_iota(jnp.int32, tail.shape, 0) == 7
+    return jnp.concatenate([moved[:-8], jnp.where(last, turned(tail, 64), tail)], 0)
+
+
 class Level:
     def __init__(self, phases, spread, rows, refs):
-        self.phases, self.spread, self.rows = phases, spread, rows
-        self.west, self.east, self.south, self.last_north, self.upper, self.inverse, self.link, self.value, self.forcing = refs
+        self.phases, self.spread, self.rows, self.folded = phases, spread, rows, rows == COARSE_ROWS
+        self.west, self.east, self.south, self.last_north, self.upper, self.gain, self.pull, self.link, self.value, self.forcing = refs
 
     @staticmethod
     def scratch(phases, rows):
         full = pltpu.VMEM((phases, NZ, rows, LANES), jnp.float32)
-        return [
-            full,
-            full,
-            full,
-            pltpu.VMEM((NZ, rows, LANES), jnp.float32),
-            pltpu.VMEM((phases, NZ + 1, rows, LANES), jnp.float32),
-            full,
-            full,
-            full,
-            full,
-        ]
+        edge = pltpu.VMEM((NZ, rows, LANES), jnp.float32)
+        column = pltpu.VMEM((phases, NZ + 1, rows, LANES), jnp.float32)
+        return [full, full, full, edge, column, full, full, full, full, full]
 
     def north(self, phase, k):
         return self.south[phase + 1, k] if phase + 1 < self.phases else self.last_north[k]
@@ -80,8 +91,8 @@
             before = values[phase - 1] if phase else turned(values[-1], self.spread)
             after = values[phase + 1] if phase + 1 < self.phases else turned(values[0], -self.spread)
             out.append(
-                self.west[phase, k] * row_turned(value, 1)
-                + self.east[phase, k] * row_turned(value, -1)
+                self.west[phase, k] * row_before(value, self.folded)
+                + self.east[phase, k] * row_after(value, self.folded)
                 + self.south[phase, k] * before
                 + self.north(phase, k) * after
             )
@@ -90,7 +101,7 @@
     def set_faces(self, k, west, south, upper):
         for phase in range(self.phases):
             self.west[phase, k] = west[phase]
-            self.east[phase, k] = row_turned(west[phase], -1)
+            self.east[phase, k] = row_after(west[phase], self.folded)
             self.south[phase, k] = south[phase]
             self.upper[phase, k] = upper[phase]
         self.last_north[k] = turned(south[0], -self.spread)
@@ -99,23 +110,6 @@
         for phase in range(self.phases):
             self.upper[phase, NZ] = jnp.zeros((self.rows, LANES), jnp.float32)
 
-    def factor(self, centre_ref=None):
-        def body(k, before):
-            now = []
-            for phase in range(self.phases):
-                upper, lower = self.upper[phase, k], self.upper[phase, k + 1]
-                centre = self.west[phase, k] + self.east[phase, k] + self.south[phase, k] + self.north(phase, k) + upper + lower
-                if centre_ref is not None:
-                    centre_ref[phase, k] = centre
-                inverse = 1.0 / jnp.maximum(centre - upper * upper * before[phase], TINY)
-                self.inverse[phase, k] = inverse
-                self.link[phase, k] = lower * inverse
-                now.append(inverse)
-            return tuple(now)
-
-        zero = jnp.zeros((self.rows, LANES), jnp.float32)
-        layers(body, (zero,) * self.phases)
-
     def start(self, held, after=None, low=0):
         rows = pl.ds(low, self.rows - low)
         zero = jnp.zeros((self.rows - low, LANES), jnp.float32)
@@ -123,22 +117,20 @@
         def down(k, before):
             now = []
             for phase in range(self.phases):
-                total = self.forcing[phase, k, rows] + self.upper[phase, k, rows] * before[phase]
-                now.append(total * self.inverse[phase, k, rows])
+                now.append(self.gain[phase, k, rows] * self.forcing[phase, k, rows] + self.pull[phase, k, rows] * before[phase])
                 held[phase, k, rows] = now[-1]
             return tuple(now)
 
         layers(down, (zero,) * self.phases)
 
         def up(k, below):
-            now, values = [], []
+            values = []
             for phase in range(self.phases):
-                now.append(held[phase, k, rows] + self.link[phase, k, rows] * below[phase])
-                values.append(relaxation * now[-1])
+                values.append(held[phase, k, rows] + self.link[phase, k, rows] * below[phase])
                 self.value[phase, k, rows] = values[-1]
             if after is not None:
                 after(k, values)
-            return tuple(now)
+            return tuple(values)
 
         layers(up, (zero,) * self.phases, reverse=True)
 
@@ -156,8 +148,7 @@
                     self.value[phase, k] = values[phase]
             now = []
             for phase, part in enumerate(self.horizontal(k, values)):
-                total = self.forcing[phase, k] + part + self.upper[phase, k] * before[phase]
-                now.append(total * self.inverse[phase, k])
+                now.append(self.gain[phase, k] * (self.forcing[phase, k] + part) + self.pull[phase, k] * before[phase])
                 held[phase, k] = now[-1]
             return tuple(now)
 
@@ -167,10 +158,31 @@
             now = []
             for phase in range(self.phases):
                 now.append(held[phase, k] + self.link[phase, k] * below[phase])
-                self.value[phase, k] = (1.0 - relaxation) * self.value[phase, k] + relaxation * now[-1]
+                self.value[phase, k] = (1.0 - relaxation) * self.value[phase, k] + now[-1]
             return tuple(now)
 
         layers(up, (zero,) * self.phases, reverse=True)
+
+
+def factor(levels, centre_ref=None):
+    def body(k, before):
+        now = []
+        for no, level in enumerate(levels):
+            links = []
+            for phase in range(level.phases):
+                upper, lower = level.upper[phase, k], level.upper[phase, k + 1]
+                centre = level.west[phase, k] + level.east[phase, k] + level.south[phase, k] + level.north(phase, k) + upper + lower
+                if no == 0 and centre_ref is not None:
+                    centre_ref[phase, k] = centre
+                inverse = 1.0 / jnp.maximum(centre - upper * before[no][phase], TINY)
+                level.gain[phase, k] = relaxation * inverse
+                level.pull[phase, k] = upper * inverse
+                links.append(lower * inverse)
+                level.link[phase, k] = links[-1]
+            now.append(tuple(links))
+        return tuple(now)
+
+    layers(body, tuple((jnp.zeros((level.rows, LANES), jnp.float32),) * level.phases for level in levels))
 
 
 def paired_lanes(values, spread, lane):
@@ -184,10 +196,11 @@
 def kernel(
     cross_count,
     along_count,
-    source_ref,
-    density_ref,
-    pressure_ref,
-    residual_ref,
+    source_hbm,
+    density_hbm,
+    pressure_hbm,
+    residual_hbm,
+    raw,
     dense,
     first_out,
     last_out,
@@ -205,13 +218,17 @@
     coarse_held,
     *rest,
 ):
-    level_refs, (fine_send, fine_recv, coarse_send, coarse_recv, fresh_send, fresh_recv) = rest[:-6], rest[-6:]
+    level_refs, (own_sem, out_sem, fine_send, fine_recv, coarse_send, coarse_recv, fresh_send, fresh_recv) = rest[:-8], rest[-8:]
     shapes = [(4, 1, FINE_ROWS), (2, 1, FINE_ROWS), (1, 1, FINE_ROWS), (1, 2, FINE_ROWS), (1, 1, COARSE_ROWS), (1, 2, COARSE_ROWS), (1, 4, COARSE_ROWS)]
-    grid = [Level(*shape, level_refs[9 * no : 9 * no + 9]) for no, shape in enumerate(shapes)]
+    grid = [Level(*shape, level_refs[10 * no : 10 * no + 10]) for no, shape in enumerate(shapes)]
     c, a = lax.axis_index("cross"), lax.axis_index("along")
 
     def inside(d, e):
         return (c + d >= 0) & (c + d < cross_count) & (a + e >= 0) & (a + e < along_count)
+
+    own_copies = [pltpu.make_async_copy(hbm, raw.at[which], own_sem.at[which]) for which, hbm in ((0, source_hbm), (1, density_hbm))]
+    for copy in own_copies[::-1]:
+        copy.start()
 
     for ref in (first_in, last_in, own_in, near_in, far_in, fresh):
         ref[...] = jnp.zeros(ref.shape, ref.dtype)
@@ -224,7 +241,9 @@
         def _(d=d, e=e):
             pl.semaphore_signal(barrier, inc=1, device_id=(c + d, a + e), device_id_type=MESH)
 
-    def own_cells(which, ref):
+    def own_cells(which):
+        own_copies[which].wait()
+        ref = raw.at[which]
         lane = lanes_of(16)
         index = (4 * (lane & 63) + (lane >> 6)) & 127
         lower = (lane & 63) < 32
@@ -277,7 +296,7 @@
         return copies
 
     def coarse_copies(which):
-        fields = pl.ds(0, 3) if which == 0 else pl.ds(3, 1)
+        fields = (pl.ds(2, 1), pl.ds(0, 2), pl.ds(3, 1))[which]
         copies = []
         for no, (d, e) in enumerate(COARSE_SIDES):
             put = pl.ds({0: 0, 1: 16, -1: 32}[e], 16)
@@ -288,7 +307,7 @@
                 src, dst = near_out.at[side, fields], near_in.at[side, fields, :, put, :]
             else:
                 side = 0 if d > 0 else 1
-                src, dst = far_out.at[fields], far_in.at[side, fields, put, :]
+                src, dst = far_out.at[side, fields], far_in.at[side, {0: 0, 1: 1, -1: 2}[e], fields]
             copies.append(
                 (
                     d,
@@ -360,23 +379,53 @@
 
             lax.fori_loop(0, 8, body, tuple(halos), unroll=True)
 
-    own_cells(1, density_ref)
+    own_cells(1)
     counted = (
         (jnp.minimum(c, 2) + jnp.minimum(cross_count - 1 - c, 2) + 1) * (jnp.minimum(a, 1) + jnp.minimum(along_count - 1 - a, 1) + 1) - 1
     )
     pl.semaphore_wait(barrier, counted)
     density_copies = fine_copies(1)
     start(density_copies)
-    own_cells(0, source_ref)
+    own_cells(0)
     source_copies = fine_copies(0)
     start(source_copies)
+    lane = lanes_of(FINE_ROWS)
+    lane_16 = lanes_of(16)
+
+    def pack(field, layer_of):
+        near_index = 4 * (lane_16 & 15)
+        far_index = 4 * ((lane_16 & 3) + 12 * (lane_16 >> 6))
+        near_slot, far_slot = lane_16 >> 4, (lane_16 & 63) >> 2
+        far = jnp.zeros((16, LANES), jnp.float32)
+        for group in range(2):
+            near = jnp.zeros((16, LANES), jnp.float32)
+            for q in range(8):
+                k = 8 * group + q
+                value = layer_of(k)
+                near = jnp.where(near_slot == q, value(near_index), near)
+                far = jnp.where(far_slot == k, value(far_index), far)
+            own_in[field, group, 0:16] = near
+            near_out[0, field, group] = turned(near, 16)
+            near_out[1, field, group] = turned(near, -16)
+        low = lanes_of(8) < 64
+        far_out[0, field] = jnp.where(low, far[0:8], turned(far[8:16], 64))
+        far_out[1, field] = jnp.where(low, turned(far[0:8], 64), far[8:16])
+
+    def own_upper(k):
+        total = jnp.zeros((16, LANES), jnp.float32)
+        for half in range(2):
+            now = dense[1, half, k, 0:16]
+            total += vertical_weight * harmonic(now, dense[1, half, k - 1, 0:16]) if k else 2.0 * vertical_weight * now
+        total = paired_lanes(total + turned(total, 64), 1, lane_16)
+        return lambda index: picked(total, index) + picked(total, index + 2)
+
+    pack(2, own_upper)
+    upper_copies = coarse_copies(0)
+    start(upper_copies)
     for level in grid:
         level.close_upper()
     arrive(density_copies)
     whole_cells(1, cells)
-
-    lane = lanes_of(FINE_ROWS)
-    lane_16 = lanes_of(16)
 
     def faces(k, above):
         now = [cells[phase, k] for phase in range(4)]
@@ -398,23 +447,6 @@
 
     layers(faces, (jnp.ones((FINE_ROWS, LANES), jnp.float32),) * 4)
 
-    def pack(field, layer_of):
-        near_index = 4 * (lane_16 & 15)
-        far_index = 4 * ((lane_16 & 3) + 12 * (lane_16 >> 6))
-        near_slot, far_slot = lane_16 >> 4, (lane_16 & 63) >> 2
-        far = jnp.zeros((16, LANES), jnp.float32)
-        for group in range(2):
-            near = jnp.zeros((16, LANES), jnp.float32)
-            for q in range(8):
-                k = 8 * group + q
-                value = layer_of(k)
-                near = jnp.where(near_slot == q, value(near_index), near)
-                far = jnp.where(far_slot == k, value(far_index), far)
-            own_in[field, group, 0:16] = near
-            near_out[0, field, group] = turned(near, 16)
-            near_out[1, field, group] = turned(near, -16)
-        far_out[field] = far
-
     def both(ref):
         def layer_of(k):
             values = ref[0, k, 0:16]
@@ -431,13 +463,10 @@
 
     pack(0, both(grid[3].west))
     pack(1, half_first(grid[3].south))
-    pack(2, both(grid[3].upper))
-    face_copies = coarse_copies(0)
+    face_copies = coarse_copies(1)
     start(face_copies)
 
-    grid[0].factor(centre)
-    for no in (1, 2, 3):
-        grid[no].factor()
+    factor(grid[:4], centre)
 
     arrive(source_copies)
     whole_cells(0, grid[0].forcing)
@@ -465,7 +494,7 @@
 
     grid[3].start(held, keep_rest)
     pack(3, both(cells))
-    forcing_copies = coarse_copies(1)
+    forcing_copies = coarse_copies(2)
     start(forcing_copies)
 
     arrive(third_copies)
@@ -478,25 +507,39 @@
     layers(renew, 0)
     grid[3].start(held, low=16)
 
-    lane_48 = lanes_of(COARSE_ROWS)
+    lane_8, lane_24 = lanes_of(8), lanes_of(COARSE_ROWS)
+    low = lane_8 < 64
 
     def unpacked(field):
-        near_slot = lane_48 >> 4
-        middle = (lane_48 >= 32) & (lane_48 < 112)
-        far = jnp.where(lane_48 < 64, far_in[0, field], far_in[1, field])
+        fars = []
+        for side in range(2):
+            tiles = []
+            for (low_no, low_half), (high_no, high_half) in (((2, 0), (0, 1)), ((2, 1), (1, 0)), ((0, 0), (1, 1))):
+                lower, higher = far_in[side, low_no, field], far_in[side, high_no, field]
+                lower = turned(lower, 64) if low_half else lower
+                higher = higher if high_half else turned(higher, 64)
+                tiles.append(jnp.where(low, lower, higher))
+            fars.append(jnp.concatenate(tiles, 0))
+        nears = []
+        for group in range(2):
+            for ref in (own_in.at[field, group], near_in.at[0, field, group], near_in.at[1, field, group]):
+                nears.append((jnp.concatenate([ref[32:48], ref[0:8]], 0), turned(ref[8:32], 64)))
+        slot, part = lane_24 >> 4, lane_24 & 63
 
         def layer_of(k):
             group, q = k // 8, k % 8
-            mixed = jnp.where(
-                near_slot == q,
-                own_in[field, group],
-                jnp.where(near_slot == (q + 1) % 8, near_in[0, field, group], near_in[1, field, group]),
-            )
-            index = jnp.where(lane_48 < 64, (4 * k + lane_48 + 32) & 63, 64 + ((4 * k + lane_48 + 20) & 63))
-            return jnp.where(middle, picked(far, index), turned(mixed, -16 * q))
+            own, after, before = nears[3 * group : 3 * group + 3]
+            at = (slot - q) & 7
+            mixed = own[0]
+            for place, tile in ((1, after[0]), (7, before[0]), (4, own[1]), (5, after[1]), (3, before[1])):
+                mixed = jnp.where(at == place, tile, mixed)
+            mixed = turned(mixed, 24 - 16 * q)
+            mixed = jnp.where(part >= 56, turned(fars[0], 56 - 4 * k), mixed)
+            return jnp.where(part < 8, turned(fars[1], 4 - 4 * k), mixed)
 
         return layer_of
 
+    arrive(upper_copies)
     arrive(face_copies)
     west_of, south_of, upper_of = unpacked(0), unpacked(1), unpacked(2)
     for k in range(NZ):
@@ -504,10 +547,9 @@
         grid[4].set_faces(k, [west], [south], [upper])
         for no in (5, 6):
             spread = grid[no].spread // 2
-            west, south, upper = paired_lanes(west, spread, lane_48), 0.5 * first_child(south, spread, lane_48), paired_lanes(upper, spread, lane_48)
+            west, south, upper = paired_lanes(west, spread, lane_24), 0.5 * first_child(south, spread, lane_24), paired_lanes(upper, spread, lane_24)
             grid[no].set_faces(k, [west], [south], [upper])
-    for no in (4, 5, 6):
-        grid[no].factor()
+    factor(grid[4:])
 
     arrive(forcing_copies)
     forcing_of = unpacked(3)
@@ -522,9 +564,12 @@
     grid[5].sweep(coarse_held, lambda k: [grid[6].value[0, k]])
     grid[4].sweep(coarse_held, lambda k: [grid[5].value[0, k]])
 
+    row = lax.broadcasted_iota(jnp.int32, (FINE_ROWS, LANES), 0)
+    third_index = jnp.where(lane < 96, (lane >> 2) + 24, (lane >> 2) - 8) + jnp.where((row >= 8) & (row < 24), 64, 0)
+
     def to_third(k):
-        values = jnp.concatenate([grid[4].value[0, k, 0:24], grid[4].value[0, k, 40:48]], 0)
-        return [picked(values, jnp.where(lane < 96, lane >> 2, (lane >> 2) + 96))]
+        values = grid[4].value[0, k]
+        return [picked(jnp.concatenate([values[16:24], values[0:16], values[8:16]], 0), third_index)]
 
     grid[3].sweep(held, to_third)
     grid[2].sweep(held, lambda k: [grid[3].value[0, k]])
@@ -536,7 +581,7 @@
         index = (lane_16 & 1) * 64 + (lane_16 >> 2)
         for tile in range(2):
             at = index + 32 * tile
-            ref[k, :, tile * LANES : (tile + 1) * LANES] = jnp.where((lane_16 & 3) < 2, picked(halves[0], at), picked(halves[1], at))
+            raw[ref, k, :, tile * LANES : (tile + 1) * LANES] = jnp.where((lane_16 & 3) < 2, picked(halves[0], at), picked(halves[1], at))
 
     fine = grid[0]
 
@@ -557,14 +602,23 @@
                 )
             )
         values = [value[0:16] for value in values]
-        laid_out(pressure_ref, k, values)
-        laid_out(residual_ref, k, rest)
+        laid_out(0, k, values)
+        laid_out(1, k, rest)
         return tuple(values)
 
-    layers(finish, (jnp.zeros((16, LANES), jnp.float32),) * 4)
-
-    for copies in (density_copies, source_copies, face_copies, third_copies, forcing_copies):
+    above = (jnp.zeros((16, LANES), jnp.float32),) * 4
+    out_copies = []
+    for part in range(2):
+        done = pl.ds(8 * part, 8)
+        above = lax.fori_loop(8 * part, 8 * part + 8, finish, above, unroll=True)
+        for which, hbm in enumerate((pressure_hbm, residual_hbm)):
+            out_copies.append(pltpu.make_async_copy(raw.at[which, done], hbm.at[done], out_sem.at[which, part]))
+            out_copies[-1].start()
+
+    for copies in (density_copies, source_copies, upper_copies, face_copies, third_copies, forcing_copies):
         leave(copies)
+    for copy in out_copies:
+        copy.wait()
 
 
 def solution(mesh):
@@ -574,16 +628,17 @@
         shape = jax.ShapeDtypeStruct(source.shape, jnp.float32)
         vmem = lambda *dims: pltpu.VMEM(dims, jnp.float32)
         scratch = [
+            vmem(2, *source.shape),
             vmem(2, 2, NZ, FINE_ROWS, LANES),
             vmem(2, 2, 2, 16, LANES),
             vmem(2, 2, 2, 16, LANES),
             vmem(2, 2, 2, FINE_ROWS, LANES),
             vmem(2, 2, 2, FINE_ROWS, LANES),
             vmem(2, 4, 2, 16, LANES),
-            vmem(4, 16, LANES),
-            vmem(4, 2, COARSE_ROWS, LANES),
-            vmem(2, 4, 2, COARSE_ROWS, LANES),
-            vmem(2, 4, COARSE_ROWS, LANES),
+            vmem(2, 4, 8, LANES),
+            vmem(4, 2, HELD_ROWS, LANES),
+            vmem(2, 4, 2, HELD_ROWS, LANES),
+            vmem(2, 3, 4, 8, LANES),
             vmem(2, NZ, 8, LANES),
             vmem(4, NZ, FINE_ROWS, LANES),
             vmem(4, NZ, FINE_ROWS, LANES),
@@ -593,18 +648,20 @@
         for phases, rows in [(4, FINE_ROWS), (2, FINE_ROWS), (1, FINE_ROWS), (1, FINE_ROWS)] + [(1, COARSE_ROWS)] * 3:
             scratch += Level.scratch(phases, rows)
         scratch += [
+            pltpu.SemaphoreType.DMA((2,)),
+            pltpu.SemaphoreType.DMA((2, 2)),
             pltpu.SemaphoreType.DMA((2, len(FINE_SIDES))),
             pltpu.SemaphoreType.DMA((2, len(FINE_SIDES))),
-            pltpu.SemaphoreType.DMA((2, len(COARSE_SIDES))),
-            pltpu.SemaphoreType.DMA((2, len(COARSE_SIDES))),
+            pltpu.SemaphoreType.DMA((3, len(COARSE_SIDES))),
+            pltpu.SemaphoreType.DMA((3, len(COARSE_SIDES))),
             pltpu.SemaphoreType.DMA((2,)),
             pltpu.SemaphoreType.DMA((2,)),
         ]
         return pl.pallas_call(
             functools.partial(kernel, cross_count, along_count),
             out_shape=(shape, shape),
-            in_specs=[pl.BlockSpec(memory_space=pltpu.VMEM)] * 2,
-            out_specs=(pl.BlockSpec(memory_space=pltpu.VMEM),) * 2,
+            in_specs=[pl.BlockSpec(memory_space=pl.ANY)] * 2,
+            out_specs=(pl.BlockSpec(memory_space=pl.ANY),) * 2,
             scratch_shapes=scratch,
             compiler_params=pltpu.CompilerParams(collective_id=0, has_side_effects=True, vmem_limit_bytes=56 * 2**20),
         )(source, density)

time: 46 us -> 37.5 us (0.82)
  Pallas kernels: 42.7 us -> 34.4 us
    pallas_call x1, Pallas kernels: 42.7 us -> 34.4 us  [per_device(): pl.pallas_call(functools.partial(kernel, cross_count, along_count), out_s...]
where the time goes in v1:
time: 37.5 us; the launch traced here: 37.4 us
  Pallas kernels  34.4 us (92%)
  local copies, waits for them, and re-layouts  2.42 us (6%)
  between operations  0.65 us (2%)
    pallas_call x1, Pallas kernels, per_device(): pl.pallas_call(functools.partial(kernel, cross_count, along_count), out_s...  34.4 us
    unnamed x4, local copies, waits for them, and re-layouts  2.42 us

profile of v1, /device:TPU:131, one launch (start us, length us, event | category | flops | bytes accessed | tf_op | source)
XLA Modules:
  0.0 37.4 jit_solution(5786980704446472364)
XLA Ops:
  0.6 34.4 %shard_map.41 = (f32[16,16,256]{2,1,0:T(8,128)}, f32[16,16,256]{2,1,0:T(8,128)}) custom-call(f32[16,16,256]{2,1,0:T(8,128)} %source_hbm.1, f32[16,16,256]{2,1,0:T(8,128)} %density_hbm.1), custom_call_target="tpu_custom_call" | custom-call | tf_op jit(solution)/shard_map/pallas_call | solution.py:660
  35.0 0.0 copy-start
  35.0 1.7 %copy.6 = f32[16,16,256]{2,1,0:T(8,128)} copy(f32[16,16,256]{2,1,0:T(8,128)} %get-tuple-element.4) | data formatting | bytes 524288
  36.7 0.0 copy-done
  36.7 0.7 %copy.7 = f32[16,16,256]{2,1,0:T(8,128)} copy(f32[16,16,256]{2,1,0:T(8,128)S(1)} %copy-done) | data formatting | bytes 524288
Async XLA Ops:
  35.0 1.7 %copy-start = (f32[16,16,256]{2,1,0:T(8,128)S(1)}, f32[16,16,256]{2,1,0:T(8,128)}, u32[]{:S(2)}) copy-start(f32[16,16,256]{2,1,0:T(8,128)} %get-tuple-element.5) | copy-start | bytes 786436

commit v2 on v1

--- a/solution.py
+++ b/solution.py
@@ -21,8 +21,8 @@
 vertical_weight = 0.5
 relaxation = 0.8
 
-COARSE_SIDES = [(d, e) for d in (0, 1, -1, 2, -2) for e in (0, 1, -1) if (d, e) != (0, 0)]
-FINE_SIDES = [(d, e) for d in (0, 1, -1) for e in (0, 1, -1) if (d, e) != (0, 0)]
+COARSE_SIDES = [(d, e) for d in (1, -1, 2, -2, 0) for e in (0, 1, -1) if (d, e) != (0, 0)]
+FINE_SIDES = [(d, e) for d in (1, -1, 0) for e in (0, 1, -1) if (d, e) != (0, 0)]
 
 
 def layers(body, init, reverse=False):
@@ -44,8 +44,9 @@
     return pltpu.roll(values, by % values.shape[0], axis=0)
 
 
-def harmonic(first, second):
-    return 2.0 * first * second / jnp.maximum(first + second, TINY)
+def harmonic(weight, first, second):
+    product = first * second if weight == 0.5 else (2.0 * weight) * first * second
+    return product * (1.0 / (first + second))
 
 
 def lanes_of(rows):
@@ -73,38 +74,32 @@
 class Level:
     def __init__(self, phases, spread, rows, refs):
         self.phases, self.spread, self.rows, self.folded = phases, spread, rows, rows == COARSE_ROWS
-        self.west, self.east, self.south, self.last_north, self.upper, self.gain, self.pull, self.link, self.value, self.forcing = refs
+        self.west, self.south, self.upper, self.gain, self.pull, self.link, self.value, self.forcing = refs
 
     @staticmethod
     def scratch(phases, rows):
         full = pltpu.VMEM((phases, NZ, rows, LANES), jnp.float32)
-        edge = pltpu.VMEM((NZ, rows, LANES), jnp.float32)
         column = pltpu.VMEM((phases, NZ + 1, rows, LANES), jnp.float32)
-        return [full, full, full, edge, column, full, full, full, full, full]
-
-    def north(self, phase, k):
-        return self.south[phase + 1, k] if phase + 1 < self.phases else self.last_north[k]
+        return [full, full, column, full, full, full, full, full]
 
     def horizontal(self, k, values):
+        rows = pl.ds(0, values[0].shape[0])
+        west = [self.west[phase, k, rows] for phase in range(self.phases)]
+        south = [self.south[phase, k, rows] for phase in range(self.phases)]
+        onward = [face * value for face, value in zip(south, values)]
         out = []
         for phase, value in enumerate(values):
             before = values[phase - 1] if phase else turned(values[-1], self.spread)
-            after = values[phase + 1] if phase + 1 < self.phases else turned(values[0], -self.spread)
-            out.append(
-                self.west[phase, k] * row_before(value, self.folded)
-                + self.east[phase, k] * row_after(value, self.folded)
-                + self.south[phase, k] * before
-                + self.north(phase, k) * after
-            )
+            north = onward[phase + 1] if phase + 1 < self.phases else turned(onward[0], -self.spread)
+            along = west[phase] * row_before(value, self.folded) + row_after(west[phase] * value, self.folded)
+            out.append(along + south[phase] * before + north)
         return out
 
     def set_faces(self, k, west, south, upper):
         for phase in range(self.phases):
             self.west[phase, k] = west[phase]
-            self.east[phase, k] = row_after(west[phase], self.folded)
             self.south[phase, k] = south[phase]
             self.upper[phase, k] = upper[phase]
-        self.last_north[k] = turned(south[0], -self.spread)
 
     def close_upper(self):
         for phase in range(self.phases):
@@ -137,28 +132,44 @@
     def remain(self, k, values):
         return [(1.0 - relaxation) * self.forcing[phase, k] + part for phase, part in enumerate(self.horizontal(k, values))]
 
-    def sweep(self, held, coarse=None):
+    def near(self):
+        first = lax.broadcasted_iota(jnp.int32, (8, LANES), 0) < 4
+
+        def body(k, _):
+            for ref in (self.west, self.south, self.gain, self.pull, self.link, self.value, self.forcing):
+                for phase in range(self.phases):
+                    ref[phase, k, 16:24] = jnp.where(first, ref[phase, k, 16:24], ref[phase, k, 24:32])
+            return 0
+
+        layers(body, 0)
+        self.rows = 24
+
+    def sweep(self, held, coarse=None, after=None):
         zero = jnp.zeros((self.rows, LANES), jnp.float32)
+        rows = pl.ds(0, self.rows)
 
         def down(k, before):
-            values = [self.value[phase, k] for phase in range(self.phases)]
+            values = [self.value[phase, k, rows] for phase in range(self.phases)]
             if coarse is not None:
                 values = [value + extra for value, extra in zip(values, coarse(k))]
                 for phase in range(self.phases):
-                    self.value[phase, k] = values[phase]
+                    self.value[phase, k, rows] = values[phase]
             now = []
             for phase, part in enumerate(self.horizontal(k, values)):
-                now.append(self.gain[phase, k] * (self.forcing[phase, k] + part) + self.pull[phase, k] * before[phase])
-                held[phase, k] = now[-1]
+                now.append(self.gain[phase, k, rows] * (self.forcing[phase, k, rows] + part) + self.pull[phase, k, rows] * before[phase])
+                held[phase, k, rows] = now[-1]
             return tuple(now)
 
         layers(down, (zero,) * self.phases)
 
         def up(k, below):
-            now = []
+            now, values = [], []
             for phase in range(self.phases):
-                now.append(held[phase, k] + self.link[phase, k] * below[phase])
-                self.value[phase, k] = (1.0 - relaxation) * self.value[phase, k] + now[-1]
+                now.append(held[phase, k, rows] + self.link[phase, k, rows] * below[phase])
+                values.append((1.0 - relaxation) * self.value[phase, k, rows] + now[-1])
+                self.value[phase, k, rows] = values[-1]
+            if after is not None:
+                after(k, values)
             return tuple(now)
 
         layers(up, (zero,) * self.phases, reverse=True)
@@ -171,7 +182,9 @@
             links = []
             for phase in range(level.phases):
                 upper, lower = level.upper[phase, k], level.upper[phase, k + 1]
-                centre = level.west[phase, k] + level.east[phase, k] + level.south[phase, k] + level.north(phase, k) + upper + lower
+                west, south = level.west[phase, k], level.south[phase, k]
+                north = level.south[phase + 1, k] if phase + 1 < level.phases else turned(level.south[0, k], -level.spread)
+                centre = west + row_after(west, level.folded) + south + north + upper + lower
                 if no == 0 and centre_ref is not None:
                     centre_ref[phase, k] = centre
                 inverse = 1.0 / jnp.maximum(centre - upper * before[no][phase], TINY)
@@ -185,11 +198,11 @@
     layers(body, tuple((jnp.zeros((level.rows, LANES), jnp.float32),) * level.phases for level in levels))
 
 
-def paired_lanes(values, spread, lane):
-    return values + picked(values, lane ^ spread)
-
-
-def first_child(values, spread, lane):
+def paired_lanes(values, spread):
+    return values + turned(values, -spread)
+
+
+def both_children(values, spread, lane):
     return jnp.where((lane & spread) == 0, values, turned(values, spread))
 
 
@@ -220,7 +233,7 @@
 ):
     level_refs, (own_sem, out_sem, fine_send, fine_recv, coarse_send, coarse_recv, fresh_send, fresh_recv) = rest[:-8], rest[-8:]
     shapes = [(4, 1, FINE_ROWS), (2, 1, FINE_ROWS), (1, 1, FINE_ROWS), (1, 2, FINE_ROWS), (1, 1, COARSE_ROWS), (1, 2, COARSE_ROWS), (1, 4, COARSE_ROWS)]
-    grid = [Level(*shape, level_refs[10 * no : 10 * no + 10]) for no, shape in enumerate(shapes)]
+    grid = [Level(*shape, level_refs[8 * no : 8 * no + 8]) for no, shape in enumerate(shapes)]
     c, a = lax.axis_index("cross"), lax.axis_index("along")
 
     def inside(d, e):
@@ -230,9 +243,13 @@
     for copy in own_copies[::-1]:
         copy.start()
 
-    for ref in (first_in, last_in, own_in, near_in, far_in, fresh):
+    for ref in (own_in, near_in, far_in, fresh):
         ref[...] = jnp.zeros(ref.shape, ref.dtype)
-    dense[:, :, :, 16:32, :] = jnp.zeros((2, 2, NZ, 16, LANES), jnp.float32)
+    dense[0, :, :, 16:32, :] = jnp.zeros((2, NZ, 16, LANES), jnp.float32)
+    dense[1, :, :, 16:32, :] = jnp.full((2, NZ, 16, LANES), TINY, jnp.float32)
+    for ref in (first_in, last_in):
+        ref[0] = jnp.zeros(ref.shape[1:], ref.dtype)
+        ref[1] = jnp.full(ref.shape[1:], TINY, ref.dtype)
 
     barrier = pltpu.get_barrier_semaphore()
     for d, e in COARSE_SIDES:
@@ -241,7 +258,7 @@
         def _(d=d, e=e):
             pl.semaphore_signal(barrier, inc=1, device_id=(c + d, a + e), device_id_type=MESH)
 
-    def own_cells(which):
+    def own_cells(which, target):
         own_copies[which].wait()
         ref = raw.at[which]
         lane = lanes_of(16)
@@ -252,18 +269,22 @@
             left, right = ref[k, :, 0:LANES], ref[k, :, LANES : 2 * LANES]
             for half in range(2):
                 at = index + 2 * half
-                dense[which, half, k, 0:16] = jnp.where(lower, picked(left, at), picked(right, at))
+                values = jnp.where(lower, picked(left, at), picked(right, at))
+                dense[which, half, k, 0:16] = values
+                target[2 * half, k, 0:16] = values
+                target[2 * half + 1, k, 0:16] = turned(values, 64)
             return 0
 
         layers(body, 0)
-        slot = (lane & 63) >> 3
+        part = lane & 63
         for half in range(2):
             for group in range(2):
                 first = last = jnp.zeros((16, LANES), jnp.float32)
                 for q in range(8):
                     values = dense[which, half, 8 * group + q, 0:16]
-                    first = jnp.where(slot == q, turned(values, 8 * q), first)
-                    last = jnp.where(slot == q, turned(values, 8 * q + 72), last)
+                    here = (part >= 7 * q) & (part < 7 * q + 7)
+                    first = jnp.where(here, turned(values, 7 * q), first)
+                    last = jnp.where(here, turned(values, 7 * q - 58), last)
                 first_out[which, half, group] = first
                 last_out[which, half, group] = last
 
@@ -357,36 +378,32 @@
 
     def whole_cells(which, target):
         lane = lanes_of(FINE_ROWS)
-        own = lane < 64
+        own = lanes_of(16) < 64
         for group in range(2):
             halos = []
             for phase in range(4):
                 first, last = first_in[which, phase // 2, group], last_in[which, phase // 2, group]
                 if phase % 2 == 0:
-                    halos.append(jnp.where(own, first, turned(last, 64)))
+                    halos.append(jnp.where(lane < 56, first, turned(last, 58)))
                 else:
-                    halos.append(jnp.where(own, turned(first, 64), last))
-
-            def body(q, halos, group=group):
-                index = jnp.where(lane < 96, (lane + 8 * q) & 63, 64 + ((lane + 8 + 8 * q) & 63))
+                    halos.append(jnp.where(lane < 56, turned(first, 64), turned(last, -6)))
+            for q in range(8):
                 k = 8 * group + q
                 for phase in range(4):
-                    values = dense[which, phase // 2, k]
-                    if phase % 2:
-                        values = turned(values, 64)
-                    target[phase, k] = jnp.where(own, values, picked(halos[phase], index))
-                return halos
-
-            lax.fori_loop(0, 8, body, tuple(halos), unroll=True)
-
-    own_cells(1)
+                    edges = turned(halos[phase], 64 - 7 * q)
+                    values = dense[which, phase // 2, k, 16:32]
+                    values = turned(values, 64) if phase % 2 else values
+                    target[phase, k, 0:16] = jnp.where(own, target[phase, k, 0:16], edges[0:16])
+                    target[phase, k, 16:32] = jnp.where(own, values, edges[16:32])
+
+    own_cells(1, cells)
     counted = (
         (jnp.minimum(c, 2) + jnp.minimum(cross_count - 1 - c, 2) + 1) * (jnp.minimum(a, 1) + jnp.minimum(along_count - 1 - a, 1) + 1) - 1
     )
     pl.semaphore_wait(barrier, counted)
     density_copies = fine_copies(1)
     start(density_copies)
-    own_cells(0)
+    own_cells(0, grid[0].forcing)
     source_copies = fine_copies(0)
     start(source_copies)
     lane = lanes_of(FINE_ROWS)
@@ -394,19 +411,18 @@
 
     def pack(field, layer_of):
         near_index = 4 * (lane_16 & 15)
-        far_index = 4 * ((lane_16 & 3) + 12 * (lane_16 >> 6))
-        near_slot, far_slot = lane_16 >> 4, (lane_16 & 63) >> 2
-        far = jnp.zeros((16, LANES), jnp.float32)
+        far_index = 16 * ((lane_16 >> 2) & 7) + (lane_16 & 3) + 12 * (lane_16 >> 6)
+        slot = lane_16 >> 4
+        fars = []
         for group in range(2):
             near = jnp.zeros((16, LANES), jnp.float32)
             for q in range(8):
-                k = 8 * group + q
-                value = layer_of(k)
-                near = jnp.where(near_slot == q, value(near_index), near)
-                far = jnp.where(far_slot == k, value(far_index), far)
+                near = jnp.where(slot == q, picked(layer_of(8 * group + q), near_index), near)
             own_in[field, group, 0:16] = near
             near_out[0, field, group] = turned(near, 16)
             near_out[1, field, group] = turned(near, -16)
+            fars.append(picked(near, far_index))
+        far = jnp.where((lane_16 & 63) < 32, fars[0], fars[1])
         low = lanes_of(8) < 64
         far_out[0, field] = jnp.where(low, far[0:8], turned(far[8:16], 64))
         far_out[1, field] = jnp.where(low, turned(far[0:8], 64), far[8:16])
@@ -415,9 +431,8 @@
         total = jnp.zeros((16, LANES), jnp.float32)
         for half in range(2):
             now = dense[1, half, k, 0:16]
-            total += vertical_weight * harmonic(now, dense[1, half, k - 1, 0:16]) if k else 2.0 * vertical_weight * now
-        total = paired_lanes(total + turned(total, 64), 1, lane_16)
-        return lambda index: picked(total, index) + picked(total, index + 2)
+            total += harmonic(vertical_weight, now, dense[1, half, k - 1, 0:16]) if k else 2.0 * vertical_weight * now
+        return paired_lanes(paired_lanes(total + turned(total, 64), 1), 2)
 
     pack(2, own_upper)
     upper_copies = coarse_copies(0)
@@ -432,37 +447,23 @@
         west, south, upper = [], [], []
         for phase in range(4):
             before = now[phase - 1] if phase else turned(now[3], 1)
-            west.append(along_weight * harmonic(now[phase], row_turned(now[phase], 1)))
-            south.append(cross_weight * harmonic(now[phase], before))
-            upper.append(vertical_weight * harmonic(now[phase], above[phase]))
+            west.append(harmonic(along_weight, now[phase], row_turned(now[phase], 1)))
+            south.append(harmonic(cross_weight, now[phase], before))
+            upper.append(harmonic(vertical_weight, now[phase], above[phase]))
         upper = [jnp.where(k == 0, 2.0 * vertical_weight * now[phase], upper[phase]) for phase in range(4)]
         grid[0].set_faces(k, west, south, upper)
         west, south, upper = [west[0] + west[1], west[2] + west[3]], [0.5 * south[0], 0.5 * south[2]], [upper[0] + upper[1], upper[2] + upper[3]]
         grid[1].set_faces(k, west, south, upper)
         west, south, upper = [west[0] + west[1]], [0.5 * south[0]], [upper[0] + upper[1]]
         grid[2].set_faces(k, west, south, upper)
-        west, south, upper = paired_lanes(west[0], 1, lane), 0.5 * first_child(south[0], 1, lane), paired_lanes(upper[0], 1, lane)
+        west, south, upper = paired_lanes(west[0], 1), 0.5 * south[0], paired_lanes(upper[0], 1)
         grid[3].set_faces(k, [west], [south], [upper])
         return tuple(now)
 
     layers(faces, (jnp.ones((FINE_ROWS, LANES), jnp.float32),) * 4)
 
-    def both(ref):
-        def layer_of(k):
-            values = ref[0, k, 0:16]
-            return lambda index: picked(values, index) + picked(values, index + 2)
-
-        return layer_of
-
-    def half_first(ref):
-        def layer_of(k):
-            values = ref[0, k, 0:16]
-            return lambda index: 0.5 * picked(values, index)
-
-        return layer_of
-
-    pack(0, both(grid[3].west))
-    pack(1, half_first(grid[3].south))
+    pack(0, lambda k: paired_lanes(grid[3].west[0, k, 0:16], 2))
+    pack(1, lambda k: 0.5 * grid[3].south[0, k, 0:16])
     face_copies = coarse_copies(1)
     start(face_copies)
 
@@ -480,7 +481,7 @@
                 for phase in range(below.phases):
                     below.forcing[phase, k] = rest[2 * phase] + rest[2 * phase + 1]
             else:
-                below.forcing[0, k] = paired_lanes(rest[0], level.spread, lanes_of(level.rows))
+                below.forcing[0, k] = paired_lanes(rest[0], level.spread)
 
         return after
 
@@ -493,7 +494,7 @@
         cells[0, k] = grid[3].remain(k, values)[0]
 
     grid[3].start(held, keep_rest)
-    pack(3, both(cells))
+    pack(3, lambda k: paired_lanes(cells[0, k, 0:16], 2))
     forcing_copies = coarse_copies(2)
     start(forcing_copies)
 
@@ -508,34 +509,32 @@
     grid[3].start(held, low=16)
 
     lane_8, lane_24 = lanes_of(8), lanes_of(COARSE_ROWS)
-    low = lane_8 < 64
 
     def unpacked(field):
-        fars = []
-        for side in range(2):
-            tiles = []
-            for (low_no, low_half), (high_no, high_half) in (((2, 0), (0, 1)), ((2, 1), (1, 0)), ((0, 0), (1, 1))):
-                lower, higher = far_in[side, low_no, field], far_in[side, high_no, field]
-                lower = turned(lower, 64) if low_half else lower
-                higher = higher if high_half else turned(higher, 64)
-                tiles.append(jnp.where(low, lower, higher))
-            fars.append(jnp.concatenate(tiles, 0))
-        nears = []
+        slot_8, part_8, inner = lane_8 >> 4, lane_8 & 3, (lane_8 & 15) < 8
+
+        def far(side, no, half, group, shift):
+            return picked(far_in[side, no, field], 64 * half + 4 * (8 * group + ((slot_8 - shift) & 7)) + part_8)
+
+        tiles = [((2, 0), (0, 1)), ((2, 1), (1, 0)), ((0, 0), (1, 1))]
+        sources = []
         for group in range(2):
-            for ref in (own_in.at[field, group], near_in.at[0, field, group], near_in.at[1, field, group]):
-                nears.append((jnp.concatenate([ref[32:48], ref[0:8]], 0), turned(ref[8:32], 64)))
-        slot, part = lane_24 >> 4, lane_24 & 63
+            places = {}
+            for place, ref in ((0, own_in.at[field, group]), (1, near_in.at[0, field, group]), (7, near_in.at[1, field, group])):
+                places[place] = jnp.concatenate([ref[32:48], ref[0:8]], 0)
+                places[(place + 4) % 8] = turned(ref[8:32], 64)
+            places[2] = jnp.concatenate([jnp.where(inner, far(0, *lower, group, 2), far(1, *higher, group, 2)) for lower, higher in tiles], 0)
+            places[6] = jnp.concatenate([jnp.where(inner, far(0, *higher, group, 6), far(1, *lower, group, 6)) for lower, higher in tiles], 0)
+            sources.append(places)
+        slot = lane_24 >> 4
 
         def layer_of(k):
-            group, q = k // 8, k % 8
-            own, after, before = nears[3 * group : 3 * group + 3]
+            places, q = sources[k // 8], k % 8
             at = (slot - q) & 7
-            mixed = own[0]
-            for place, tile in ((1, after[0]), (7, before[0]), (4, own[1]), (5, after[1]), (3, before[1])):
-                mixed = jnp.where(at == place, tile, mixed)
-            mixed = turned(mixed, 24 - 16 * q)
-            mixed = jnp.where(part >= 56, turned(fars[0], 56 - 4 * k), mixed)
-            return jnp.where(part < 8, turned(fars[1], 4 - 4 * k), mixed)
+            mixed = places[0]
+            for place in range(1, 8):
+                mixed = jnp.where(at == place, places[place], mixed)
+            return turned(mixed, 24 - 16 * q)
 
         return layer_of
 
@@ -547,9 +546,11 @@
         grid[4].set_faces(k, [west], [south], [upper])
         for no in (5, 6):
             spread = grid[no].spread // 2
-            west, south, upper = paired_lanes(west, spread, lane_24), 0.5 * first_child(south, spread, lane_24), paired_lanes(upper, spread, lane_24)
+            west, south, upper = paired_lanes(west, spread), 0.5 * south, paired_lanes(upper, spread)
             grid[no].set_faces(k, [west], [south], [upper])
     factor(grid[4:])
+    for level in grid[:3]:
+        level.near()
 
     arrive(forcing_copies)
     forcing_of = unpacked(3)
@@ -561,8 +562,8 @@
     grid[6].start(coarse_held)
     for _ in range(SWEEPS - 1):
         grid[6].sweep(coarse_held)
-    grid[5].sweep(coarse_held, lambda k: [grid[6].value[0, k]])
-    grid[4].sweep(coarse_held, lambda k: [grid[5].value[0, k]])
+    grid[5].sweep(coarse_held, lambda k: [both_children(grid[6].value[0, k], 2, lane_24)])
+    grid[4].sweep(coarse_held, lambda k: [both_children(grid[5].value[0, k], 1, lane_24)])
 
     row = lax.broadcasted_iota(jnp.int32, (FINE_ROWS, LANES), 0)
     third_index = jnp.where(lane < 96, (lane >> 2) + 24, (lane >> 2) - 8) + jnp.where((row >= 8) & (row < 24), 64, 0)
@@ -572,10 +573,15 @@
         return [picked(jnp.concatenate([values[16:24], values[0:16], values[8:16]], 0), third_index)]
 
     grid[3].sweep(held, to_third)
-    grid[2].sweep(held, lambda k: [grid[3].value[0, k]])
-    grid[1].sweep(held, lambda k: [grid[2].value[0, k]] * 2)
-    grid[0].sweep(held, lambda k: [grid[1].value[phase // 2, k] for phase in range(4)])
-
+    first = lax.broadcasted_iota(jnp.int32, (8, LANES), 0) < 4
+
+    def to_second(k):
+        values = grid[3].value[0, k]
+        values = jnp.concatenate([values[0:16], jnp.where(first, values[16:24], values[24:32])], 0)
+        return [both_children(values, 1, lane_24)]
+
+    grid[2].sweep(held, to_second)
+    grid[1].sweep(held, lambda k: [grid[2].value[0, k, 0:24]] * 2)
     def laid_out(ref, k, phases):
         halves = [jnp.where(lane_16 < 64, phases[2 * half], turned(phases[2 * half + 1], 64)) for half in range(2)]
         index = (lane_16 & 1) * 64 + (lane_16 >> 2)
@@ -584,9 +590,12 @@
             raw[ref, k, :, tile * LANES : (tile + 1) * LANES] = jnp.where((lane_16 & 3) < 2, picked(halves[0], at), picked(halves[1], at))
 
     fine = grid[0]
+    grid[0].sweep(held, lambda k: [grid[1].value[phase // 2, k, 0:24] for phase in range(4)], lambda k, values: laid_out(0, k, [value[0:16] for value in values]))
+    out_copies = [pltpu.make_async_copy(raw.at[0], pressure_hbm, out_sem.at[0, 0])]
+    out_copies[0].start()
 
     def finish(k, above):
-        values = [fine.value[phase, k] for phase in range(4)]
+        values = [fine.value[phase, k, 0:24] for phase in range(4)]
         next_k = jnp.minimum(k + 1, NZ - 1)
         rest = []
         for phase, part in enumerate(fine.horizontal(k, values)):
@@ -602,23 +611,25 @@
                 )
             )
         values = [value[0:16] for value in values]
-        laid_out(0, k, values)
         laid_out(1, k, rest)
         return tuple(values)
 
     above = (jnp.zeros((16, LANES), jnp.float32),) * 4
-    out_copies = []
     for part in range(2):
         done = pl.ds(8 * part, 8)
         above = lax.fori_loop(8 * part, 8 * part + 8, finish, above, unroll=True)
-        for which, hbm in enumerate((pressure_hbm, residual_hbm)):
-            out_copies.append(pltpu.make_async_copy(raw.at[which, done], hbm.at[done], out_sem.at[which, part]))
-            out_copies[-1].start()
+        out_copies.append(pltpu.make_async_copy(raw.at[1, done], residual_hbm.at[done], out_sem.at[1, part]))
+        out_copies[-1].start()
 
     for copies in (density_copies, source_copies, upper_copies, face_copies, third_copies, forcing_copies):
         leave(copies)
     for copy in out_copies:
         copy.wait()
+
+
+def hand_on(pressure_in, residual_in, pressure_out, residual_out):
+    pressure_out[...] = pressure_in[...]
+    residual_out[...] = residual_in[...]
 
 
 def solution(mesh):
@@ -657,7 +668,7 @@
             pltpu.SemaphoreType.DMA((2,)),
             pltpu.SemaphoreType.DMA((2,)),
         ]
-        return pl.pallas_call(
+        pressure, residual = pl.pallas_call(
             functools.partial(kernel, cross_count, along_count),
             out_shape=(shape, shape),
             in_specs=[pl.BlockSpec(memory_space=pl.ANY)] * 2,
@@ -665,6 +676,12 @@
             scratch_shapes=scratch,
             compiler_params=pltpu.CompilerParams(collective_id=0, has_side_effects=True, vmem_limit_bytes=56 * 2**20),
         )(source, density)
+        return pl.pallas_call(
+            hand_on,
+            out_shape=(shape, shape),
+            in_specs=[pl.BlockSpec(memory_space=pltpu.VMEM)] * 2,
+            out_specs=(pl.BlockSpec(memory_space=pltpu.VMEM),) * 2,
+        )(pressure, residual)
 
     return jax.shard_map(
         per_device,

time: 37.5 us -> 32 us (0.85)
  Pallas kernels: 34.4 us -> 31.3 us
  local copies, waits for them, and re-layouts: 2.42 us -> 0 us
    pallas_call x1, Pallas kernels: 34.4 us -> 29.4 us  [per_device(): pl.pallas_call(functools.partial(kernel, cross_count, along_count), out_s...]
    unnamed x4 -> x0, local copies, waits for them, and re-layouts: 2.42 us -> none
    pallas_call x0 -> x1, Pallas kernels: none -> 1.84 us  [per_device(): pl.pallas_call(hand_on, out_shape=(shape, shape), in_specs=[pl.BlockSpec(...]
where the time goes in v2:
time: 32 us; the launch traced here: 31.9 us
  Pallas kernels  31.3 us (98%)
  between operations  0.64 us (2%)
    pallas_call x1, Pallas kernels, per_device(): pl.pallas_call(functools.partial(kernel, cross_count, along_count), out_s...  29.4 us
    pallas_call x1, Pallas kernels, per_device(): pl.pallas_call(hand_on, out_shape=(shape, shape), in_specs=[pl.BlockSpec(...  1.84 us

profile of v2, /device:TPU:131, one launch (start us, length us, event | category | flops | bytes accessed | tf_op | source)
XLA Modules:
  0.0 31.9 jit_solution(2173127563247904769)
XLA Ops:
  0.6 29.4 %shard_map.41 = (f32[16,16,256]{2,1,0:T(8,128)}, f32[16,16,256]{2,1,0:T(8,128)}) custom-call(f32[16,16,256]{2,1,0:T(8,128)} %source_hbm.1, f32[16,16,256]{2,1,0:T(8,128)} %density_hbm.1), custom_call_target="tpu_custom_call" | custom-call | tf_op jit(solution)/shard_map/pallas_call | solution.py:671
  30.1 1.8 %shard_map.42 = (f32[16,16,256]{2,1,0:T(8,128)}, f32[16,16,256]{2,1,0:T(8,128)}) custom-call(f32[16,16,256]{2,1,0:T(8,128)} %get-tuple-element.4.pressure_in, f32[16,16,256]{2,1,0:T(8,128)} %get-tuple-element.5.residual_in), custom_call_target="tpu_custom_call" | custom-call | tf_op jit(solution)/shard_map/pallas_call | solution.py:679

commit v3 on v2

--- a/solution.py
+++ b/solution.py
@@ -211,8 +211,8 @@
     along_count,
     source_hbm,
     density_hbm,
-    pressure_hbm,
-    residual_hbm,
+    pressure_ref,
+    residual_ref,
     raw,
     dense,
     first_out,
@@ -231,7 +231,7 @@
     coarse_held,
     *rest,
 ):
-    level_refs, (own_sem, out_sem, fine_send, fine_recv, coarse_send, coarse_recv, fresh_send, fresh_recv) = rest[:-8], rest[-8:]
+    level_refs, (own_sem, fine_send, fine_recv, coarse_send, coarse_recv, fresh_send, fresh_recv) = rest[:-7], rest[-7:]
     shapes = [(4, 1, FINE_ROWS), (2, 1, FINE_ROWS), (1, 1, FINE_ROWS), (1, 2, FINE_ROWS), (1, 1, COARSE_ROWS), (1, 2, COARSE_ROWS), (1, 4, COARSE_ROWS)]
     grid = [Level(*shape, level_refs[8 * no : 8 * no + 8]) for no, shape in enumerate(shapes)]
     c, a = lax.axis_index("cross"), lax.axis_index("along")
@@ -243,13 +243,15 @@
     for copy in own_copies[::-1]:
         copy.start()
 
-    for ref in (own_in, near_in, far_in, fresh):
-        ref[...] = jnp.zeros(ref.shape, ref.dtype)
-    dense[0, :, :, 16:32, :] = jnp.zeros((2, NZ, 16, LANES), jnp.float32)
-    dense[1, :, :, 16:32, :] = jnp.full((2, NZ, 16, LANES), TINY, jnp.float32)
-    for ref in (first_in, last_in):
-        ref[0] = jnp.zeros(ref.shape[1:], ref.dtype)
-        ref[1] = jnp.full(ref.shape[1:], TINY, ref.dtype)
+    @pl.when((c < 2) | (c > cross_count - 3) | (a < 1) | (a > along_count - 2))
+    def _():
+        for ref in (own_in, near_in, far_in, fresh):
+            ref[...] = jnp.zeros(ref.shape, ref.dtype)
+        dense[0, :, :, 16:32, :] = jnp.zeros((2, NZ, 16, LANES), jnp.float32)
+        dense[1, :, :, 16:32, :] = jnp.full((2, NZ, 16, LANES), TINY, jnp.float32)
+        for ref in (first_in, last_in):
+            ref[0] = jnp.zeros(ref.shape[1:], ref.dtype)
+            ref[1] = jnp.full(ref.shape[1:], TINY, ref.dtype)
 
     barrier = pltpu.get_barrier_semaphore()
     for d, e in COARSE_SIDES:
@@ -587,12 +589,10 @@
         index = (lane_16 & 1) * 64 + (lane_16 >> 2)
         for tile in range(2):
             at = index + 32 * tile
-            raw[ref, k, :, tile * LANES : (tile + 1) * LANES] = jnp.where((lane_16 & 3) < 2, picked(halves[0], at), picked(halves[1], at))
+            ref[k, :, tile * LANES : (tile + 1) * LANES] = jnp.where((lane_16 & 3) < 2, picked(halves[0], at), picked(halves[1], at))
 
     fine = grid[0]
-    grid[0].sweep(held, lambda k: [grid[1].value[phase // 2, k, 0:24] for phase in range(4)], lambda k, values: laid_out(0, k, [value[0:16] for value in values]))
-    out_copies = [pltpu.make_async_copy(raw.at[0], pressure_hbm, out_sem.at[0, 0])]
-    out_copies[0].start()
+    grid[0].sweep(held, lambda k: [grid[1].value[phase // 2, k, 0:24] for phase in range(4)], lambda k, values: laid_out(pressure_ref, k, [value[0:16] for value in values]))
 
     def finish(k, above):
         values = [fine.value[phase, k, 0:24] for phase in range(4)]
@@ -611,25 +611,13 @@
                 )
             )
         values = [value[0:16] for value in values]
-        laid_out(1, k, rest)
+        laid_out(residual_ref, k, rest)
         return tuple(values)
 
-    above = (jnp.zeros((16, LANES), jnp.float32),) * 4
-    for part in range(2):
-        done = pl.ds(8 * part, 8)
-        above = lax.fori_loop(8 * part, 8 * part + 8, finish, above, unroll=True)
-        out_copies.append(pltpu.make_async_copy(raw.at[1, done], residual_hbm.at[done], out_sem.at[1, part]))
-        out_copies[-1].start()
+    layers(finish, (jnp.zeros((16, LANES), jnp.float32),) * 4)
 
     for copies in (density_copies, source_copies, upper_copies, face_copies, third_copies, forcing_copies):
         leave(copies)
-    for copy in out_copies:
-        copy.wait()
-
-
-def hand_on(pressure_in, residual_in, pressure_out, residual_out):
-    pressure_out[...] = pressure_in[...]
-    residual_out[...] = residual_in[...]
 
 
 def solution(mesh):
@@ -660,7 +648,6 @@
             scratch += Level.scratch(phases, rows)
         scratch += [
             pltpu.SemaphoreType.DMA((2,)),
-            pltpu.SemaphoreType.DMA((2, 2)),
             pltpu.SemaphoreType.DMA((2, len(FINE_SIDES))),
             pltpu.SemaphoreType.DMA((2, len(FINE_SIDES))),
             pltpu.SemaphoreType.DMA((3, len(COARSE_SIDES))),
@@ -670,18 +657,13 @@
         ]
         pressure, residual = pl.pallas_call(
             functools.partial(kernel, cross_count, along_count),
-            out_shape=(shape, shape),
+            out_shape=(pltpu.VMEM(shape.shape, shape.dtype),) * 2,
             in_specs=[pl.BlockSpec(memory_space=pl.ANY)] * 2,
-            out_specs=(pl.BlockSpec(memory_space=pl.ANY),) * 2,
+            out_specs=(pl.BlockSpec(memory_space=pltpu.VMEM),) * 2,
             scratch_shapes=scratch,
             compiler_params=pltpu.CompilerParams(collective_id=0, has_side_effects=True, vmem_limit_bytes=56 * 2**20),
         )(source, density)
-        return pl.pallas_call(
-            hand_on,
-            out_shape=(shape, shape),
-            in_specs=[pl.BlockSpec(memory_space=pltpu.VMEM)] * 2,
-            out_specs=(pl.BlockSpec(memory_space=pltpu.VMEM),) * 2,
-        )(pressure, residual)
+        return pressure, residual
 
     return jax.shard_map(
         per_device,

time: 32 us -> 30.8 us (0.963)
  Pallas kernels: 31.3 us -> 28.7 us
  local copies, waits for them, and re-layouts: 0 us -> 1.41 us
    pallas_call x1 -> x0, Pallas kernels: 1.84 us -> none  [per_device(): pl.pallas_call(hand_on, out_shape=(shape, shape), in_specs=[pl.BlockSpec(...]
    unnamed x0 -> x2, local copies, waits for them, and re-layouts: none -> 1.41 us
    pallas_call x1, Pallas kernels: 29.4 us -> 28.7 us  [per_device(): pl.pallas_call(functools.partial(kernel, cross_count, along_count), out_s...]
where the time goes in v3:
time: 30.8 us; the launch traced here: 30.7 us
  Pallas kernels  28.7 us (93%)
  local copies, waits for them, and re-layouts  1.41 us (5%)
  between operations  0.64 us (2%)
    pallas_call x1, Pallas kernels, per_device(): pl.pallas_call(functools.partial(kernel, cross_count, along_count), out_s...  28.7 us
    unnamed x2, local copies, waits for them, and re-layouts  1.41 us

profile of v3, /device:TPU:131, one launch (start us, length us, event | category | flops | bytes accessed | tf_op | source)
XLA Modules:
  0.0 30.7 jit_solution(3041080232570621923)
XLA Ops:
  0.6 28.7 %shard_map.41 = (f32[16,16,256]{2,1,0:T(8,128)S(1)}, f32[16,16,256]{2,1,0:T(8,128)S(1)}) custom-call(f32[16,16,256]{2,1,0:T(8,128)} %source_hbm.1, f32[16,16,256]{2,1,0:T(8,128)} %density_hbm.1), custom_call_target="tpu_custom_call" | custom-call | tf_op jit(solution)/shard_map/pallas_call | solution.py:658
  29.3 0.7 %copy.6 = f32[16,16,256]{2,1,0:T(8,128)} copy(f32[16,16,256]{2,1,0:T(8,128)S(1)} %get-tuple-element.2) | data formatting | bytes 524288
  30.0 0.7 %copy.7 = f32[16,16,256]{2,1,0:T(8,128)} copy(f32[16,16,256]{2,1,0:T(8,128)S(1)} %get-tuple-element.3) | data formatting | bytes 524288

commit v4 on v3

--- a/solution.py
+++ b/solution.py
@@ -21,7 +21,7 @@
 vertical_weight = 0.5
 relaxation = 0.8
 
-COARSE_SIDES = [(d, e) for d in (1, -1, 2, -2, 0) for e in (0, 1, -1) if (d, e) != (0, 0)]
+COARSE_SIDES = [(d, e) for d in (2, -2, 1, -1, 0) for e in (0, 1, -1) if (d, e) != (0, 0)]
 FINE_SIDES = [(d, e) for d in (1, -1, 0) for e in (0, 1, -1) if (d, e) != (0, 0)]
 
 
@@ -554,6 +554,8 @@
     for level in grid[:3]:
         level.near()
 
+    for copies in (density_copies, source_copies, upper_copies, face_copies, third_copies):
+        leave(copies)
     arrive(forcing_copies)
     forcing_of = unpacked(3)
     for k in range(NZ):
@@ -616,8 +618,7 @@
 
     layers(finish, (jnp.zeros((16, LANES), jnp.float32),) * 4)
 
-    for copies in (density_copies, source_copies, upper_copies, face_copies, third_copies, forcing_copies):
-        leave(copies)
+    leave(forcing_copies)
 
 
 def solution(mesh):

time: 30.8 us -> 30.7 us (level)
  no operation moved by 1% of the time
where the time goes in v4:
time: 30.7 us; the launch traced here: 30.6 us
  Pallas kernels  28.5 us (93%)
  local copies, waits for them, and re-layouts  1.41 us (5%)
  between operations  0.64 us (2%)
    pallas_call x1, Pallas kernels, per_device(): pl.pallas_call(functools.partial(kernel, cross_count, along_count), out_s...  28.5 us
    unnamed x2, local copies, waits for them, and re-layouts  1.41 us

profile of v4, /device:TPU:131, one launch (start us, length us, event | category | flops | bytes accessed | tf_op | source)
XLA Modules:
  0.0 30.6 jit_solution(18003444764796058245)
XLA Ops:
  0.6 28.5 %shard_map.41 = (f32[16,16,256]{2,1,0:T(8,128)S(1)}, f32[16,16,256]{2,1,0:T(8,128)S(1)}) custom-call(f32[16,16,256]{2,1,0:T(8,128)} %source_hbm.1, f32[16,16,256]{2,1,0:T(8,128)} %density_hbm.1), custom_call_target="tpu_custom_call" | custom-call | tf_op jit(solution)/shard_map/pallas_call | solution.py:659
  29.2 0.7 %copy.6 = f32[16,16,256]{2,1,0:T(8,128)} copy(f32[16,16,256]{2,1,0:T(8,128)S(1)} %get-tuple-element.2) | data formatting | bytes 524288
  29.9 0.7 %copy.7 = f32[16,16,256]{2,1,0:T(8,128)} copy(f32[16,16,256]{2,1,0:T(8,128)S(1)} %get-tuple-element.3) | data formatting | bytes 524288
